TPU v7x, 32 devices: a whole 2x2x4 slice. The times are simulated.
32 devices in a mesh: seq: 2 (over y), ctx: 4 (over x, core), wt: 4 (over z).
Axes of the slice: x: 2, y: 2, z: 4, core: 2. Of those that a mesh axis runs over, the one named last changes fastest.
Arguments:
- tokens: bfloat16 [16, 1024, 768], P(('seq', 'wt'), 'ctx'), may hold values from -6 to 6
- cotangent: bfloat16 [16, 1024, 768], P(('seq', 'wt'), 'ctx'), may hold values from -6 to 6
- segment_ids: int32 [16, 1024], P(('seq', 'wt'), 'ctx'), may hold values from 0 to 4, as said below
- lengths: int32 [16, 4], P(('seq', 'wt')), may hold values from 32 to 928, as said below
- w_query: bfloat16 [768, 768], P('wt'), may hold values from -0.21875 to 0.21875
- b_query: bfloat16 [768], P('wt'), may hold values from -3 to 3
- w_key: bfloat16 [768, 768], P('wt'), may hold values from -0.21875 to 0.21875
- w_value: bfloat16 [768, 768], P('wt'), may hold values from -0.21875 to 0.21875
- b_value: bfloat16 [768], P('wt'), may hold values from -3 to 3
- w_attn: bfloat16 [768, 768], P('wt'), may hold values from -1.75 to 1.75
- b_attn: bfloat16 [768], P('wt'), may hold values from -2 to 2
- ln1_gain: bfloat16 [768], P('wt'), may hold values from 0.5 to 1.5
- ln1_shift: bfloat16 [768], P('wt'), may hold values from -2 to 2
- w_inner: bfloat16 [768, 3072], P('wt'), may hold values from -0.21875 to 0.21875
- b_inner: bfloat16 [3072], P('wt'), may hold values from -3 to 3
- w_outer: bfloat16 [3072, 768], P('wt'), may hold values from -0.109375 to 0.109375
- b_outer: bfloat16 [768], P('wt'), may hold values from -2 to 2
- ln2_gain: bfloat16 [768], P('wt'), may hold values from 0.5 to 1.5
- ln2_shift: bfloat16 [768], P('wt'), may hold values from -2 to 2
Outputs:
- layer_out: bfloat16 [16, 1024, 768], P(('seq', 'wt'), 'ctx')
- grad_input: bfloat16 [16, 1024, 768], P(('seq', 'wt'), 'ctx')
- grad_w_query: float32 [768, 768], P('wt')
- grad_b_query: float32 [768], P('wt')
- grad_w_key: float32 [768, 768], P('wt')
- grad_w_value: float32 [768, 768], P('wt')
- grad_b_value: float32 [768], P('wt')
- grad_w_attn: float32 [768, 768], P('wt')
- grad_b_attn: float32 [768], P('wt')
- grad_ln1_gain: float32 [768], P('wt')
- grad_ln1_shift: float32 [768], P('wt')
- grad_w_inner: float32 [768, 3072], P('wt')
- grad_b_inner: float32 [3072], P('wt')
- grad_w_outer: float32 [3072, 768], P('wt')
- grad_b_outer: float32 [768], P('wt')
- grad_ln2_gain: float32 [768], P('wt')
- grad_ln2_shift: float32 [768], P('wt')
Inputs may be any that keep to these rules, and one draw needn't show every extreme that they name: `lengths`: the 4 documents of a sequence lie end to end from its first position, and the positions after them are padding; among the 2 sequences that one device holds, one has a single document of 1024 - 3 * max(1, 32) positions, at a place among its documents that varies, and its other documents have max(1, 32) positions each; every other sequence has documents of 64 to 256 positions. `segment_ids`: position t holds d + 1 where it lies in the sequence's document d (counted from 0 in the order of lengths), and 0 in the padding.
All inputs are finite; a program needn't handle non-finite values.
Results may differ from a plain program's by a relative error of at most 0.02.
Values may be sent and summed in bfloat16 or wider, within the bound.
No kernel may reach another device: no remote copies, remote signals or barrier semaphores. Data moves between devices by JAX's collectives and lax.ppermute only.
A program may use at most 320 MiB of HBM per device.

v0:
```python
import math
import jax
import jax.numpy as jnp
from jax import lax
from jax.sharding import PartitionSpec as P

H = 12
HD = 64
NEG = -1000000000.0
EPS = 1e-05


def product(former, latter):
    return jnp.dot(former, latter, preferred_element_type=jnp.float32)


def over_rows(former, latter):
    return lax.dot_general(
        former, latter, (((0,), (0,)), ((), ())), preferred_element_type=jnp.float32
    )


def against(former, latter):
    return lax.dot_general(
        former, latter, (((1,), (1,)), ((), ())), preferred_element_type=jnp.float32
    )


def norm_rows(values, gain, shift):
    center = jnp.mean(values, axis=-1, keepdims=True)
    offset = values - center
    spread = jnp.mean(offset * offset, axis=-1, keepdims=True)
    return offset * lax.rsqrt(spread + EPS) * gain + shift


def exact_gelu(values):
    return jax.nn.gelu(values, approximate=False)


def key_segments(doc_lens, length):
    doc_ends = jnp.cumsum(doc_lens, axis=-1)
    places = jnp.arange(length, dtype=jnp.int32)
    passed = jnp.sum((places[None, :, None] >= doc_ends[:, None, :]).astype(jnp.int32), axis=-1)
    return jnp.where(places[None, :] < doc_ends[:, -1:], passed + 1, 0)


def to_items(matrix, groups):
    seq_count, length, model_width = matrix.shape
    per_group = model_width // (groups * HD)
    shaped = matrix.reshape(seq_count, length, groups, per_group, HD)
    return shaped.transpose(0, 2, 3, 1, 4).reshape(seq_count * groups, per_group, length, HD)


def from_items(blocks, seq_count):
    count_items, per_group, length, head_size = blocks.shape
    groups = count_items // seq_count
    shaped = blocks.reshape(seq_count, groups, per_group, length, head_size)
    return shaped.transpose(0, 3, 1, 2, 4).reshape(
        seq_count, length, groups * per_group * head_size
    )


def masked_scores(head_q, head_k, q_seg, k_seg, factor):
    scores = jnp.einsum("hqd,hkd->hqk", head_q, head_k, preferred_element_type=jnp.float32) * factor
    matching = q_seg[:, None] == k_seg[None, :]
    return jnp.where(matching[None], scores, NEG)


def body(
    tokens,
    cotangent,
    segment_ids,
    lengths,
    w_query,
    b_query,
    w_key,
    w_value,
    b_value,
    w_attn,
    b_attn,
    ln1_gain,
    ln1_shift,
    w_inner,
    b_inner,
    w_outer,
    b_outer,
    ln2_gain,
    ln2_shift,
):
    shards = (
        w_query,
        b_query,
        w_key,
        w_value,
        b_value,
        w_attn,
        b_attn,
        ln1_gain,
        ln1_shift,
        w_inner,
        b_inner,
        w_outer,
        b_outer,
        ln2_gain,
        ln2_shift,
    )
    seq_count, shard_len, model_width = tokens.shape
    row_count = seq_count * shard_len
    groups = H // math.gcd(H, 4)
    factor = 1.0 / math.sqrt(HD)
    full = (
        lax.all_gather(shards[0], "wt", axis=0, tiled=True),
        lax.all_gather(shards[1], "wt", axis=0, tiled=True),
        lax.all_gather(shards[2], "wt", axis=0, tiled=True),
        lax.all_gather(shards[3], "wt", axis=0, tiled=True),
        lax.all_gather(shards[4], "wt", axis=0, tiled=True),
        lax.all_gather(shards[5], "wt", axis=0, tiled=True),
        lax.all_gather(shards[6], "wt", axis=0, tiled=True),
        lax.all_gather(shards[7], "wt", axis=0, tiled=True),
        lax.all_gather(shards[8], "wt", axis=0, tiled=True),
        lax.all_gather(shards[9], "wt", axis=0, tiled=True),
        lax.all_gather(shards[10], "wt", axis=0, tiled=True),
        lax.all_gather(shards[11], "wt", axis=0, tiled=True),
        lax.all_gather(shards[12], "wt", axis=0, tiled=True),
        lax.all_gather(shards[13], "wt", axis=0, tiled=True),
        lax.all_gather(shards[14], "wt", axis=0, tiled=True),
    )
    rows = tokens.reshape(row_count, model_width)
    query = (product(rows, full[0]) + full[1].astype(jnp.float32)).astype(jnp.bfloat16)
    key_rows = product(rows, full[2]).astype(jnp.bfloat16)
    value_rows = (product(rows, full[3]) + full[4].astype(jnp.float32)).astype(jnp.bfloat16)
    local_kv = (
        key_rows.reshape(seq_count, shard_len, model_width),
        value_rows.reshape(seq_count, shard_len, model_width),
    )
    whole_kv = (
        lax.all_gather(local_kv[0], "ctx", axis=1, tiled=True),
        lax.all_gather(local_kv[1], "ctx", axis=1, tiled=True),
    )
    seq_len = whole_kv[0].shape[1]
    key_segs = jnp.repeat(key_segments(lengths, seq_len), groups, axis=0)
    query_segs = jnp.repeat(segment_ids, groups, axis=0)
    query_items = to_items(query.reshape(seq_count, shard_len, model_width), groups)
    key_items = to_items(whole_kv[0], groups)
    value_items = to_items(whole_kv[1], groups)

    def attend(item):
        head_q, head_k, head_v, q_seg, k_seg = item
        scores = masked_scores(head_q, head_k, q_seg, k_seg, factor)
        highest = jnp.max(scores, axis=-1, keepdims=True)
        totals = jnp.sum(jnp.exp(scores - highest), axis=-1, keepdims=True)
        log_sum = highest + jnp.log(totals)
        probs = jnp.exp(scores - log_sum).astype(jnp.bfloat16)
        mixed = jnp.einsum("hqk,hkd->hqd", probs, head_v, preferred_element_type=jnp.float32)
        return (mixed, log_sum[..., 0])

    attn_items, log_sums = lax.map(
        attend, (query_items, key_items, value_items, query_segs, key_segs)
    )
    attn = from_items(attn_items, seq_count).reshape(row_count, model_width).astype(jnp.bfloat16)
    first_sum = rows.astype(jnp.float32) + product(attn, full[5]) + full[6].astype(jnp.float32)
    hidden, first_pull = jax.vjp(
        norm_rows, first_sum, full[7].astype(jnp.float32), full[8].astype(jnp.float32)
    )
    hidden_low = hidden.astype(jnp.bfloat16)
    inner = product(hidden_low, full[9]) + full[10].astype(jnp.float32)
    active, gelu_pull = jax.vjp(exact_gelu, inner)
    active_low = active.astype(jnp.bfloat16)
    second_sum = hidden + product(active_low, full[11]) + full[12].astype(jnp.float32)
    result, second_pull = jax.vjp(
        norm_rows, second_sum, full[13].astype(jnp.float32), full[14].astype(jnp.float32)
    )
    layer_out = result.astype(jnp.bfloat16).reshape(tokens.shape)
    back = (
        lax.all_gather(shards[0], "wt", axis=0, tiled=True),
        lax.all_gather(shards[1], "wt", axis=0, tiled=True),
        lax.all_gather(shards[2], "wt", axis=0, tiled=True),
        lax.all_gather(shards[3], "wt", axis=0, tiled=True),
        lax.all_gather(shards[4], "wt", axis=0, tiled=True),
        lax.all_gather(shards[5], "wt", axis=0, tiled=True),
        lax.all_gather(shards[6], "wt", axis=0, tiled=True),
        lax.all_gather(shards[7], "wt", axis=0, tiled=True),
        lax.all_gather(shards[8], "wt", axis=0, tiled=True),
        lax.all_gather(shards[9], "wt", axis=0, tiled=True),
        lax.all_gather(shards[10], "wt", axis=0, tiled=True),
        lax.all_gather(shards[11], "wt", axis=0, tiled=True),
        lax.all_gather(shards[12], "wt", axis=0, tiled=True),
        lax.all_gather(shards[13], "wt", axis=0, tiled=True),
        lax.all_gather(shards[14], "wt", axis=0, tiled=True),
    )
    back_kv = (
        lax.all_gather(local_kv[0], "ctx", axis=1, tiled=True),
        lax.all_gather(local_kv[1], "ctx", axis=1, tiled=True),
    )
    back_keys = to_items(back_kv[0], groups)
    back_values = to_items(back_kv[1], groups)
    live = (segment_ids != 0).astype(jnp.float32).reshape(row_count, 1)
    grad_rows = cotangent.reshape(row_count, model_width).astype(jnp.float32) * live
    d_second, d_gain_two, d_shift_two = second_pull(grad_rows)
    d_outer = d_second.astype(jnp.bfloat16)
    g_w_outer = over_rows(active_low, d_outer)
    g_b_outer = jnp.sum(d_outer.astype(jnp.float32), axis=0)
    d_inner = gelu_pull(against(d_outer, back[11]))[0].astype(jnp.bfloat16)
    g_w_inner = over_rows(hidden_low, d_inner)
    g_b_inner = jnp.sum(d_inner.astype(jnp.float32), axis=0)
    d_hidden = d_second + against(d_inner, back[9])
    d_first, d_gain_one, d_shift_one = first_pull(d_hidden)
    d_proj = d_first.astype(jnp.bfloat16)
    g_w_attn = over_rows(attn, d_proj)
    g_b_attn = jnp.sum(d_proj.astype(jnp.float32), axis=0)
    d_attn = against(d_proj, back[5]).astype(jnp.bfloat16)
    d_attn_seq = d_attn.reshape(seq_count, shard_len, model_width)
    d_items = to_items(d_attn_seq, groups)

    def attend_back(item):
        head_q, head_k, head_v, q_seg, k_seg, log_sum, head_d = item
        scores = masked_scores(head_q, head_k, q_seg, k_seg, factor)
        probs = jnp.exp(scores - log_sum[..., None])
        d_probs = jnp.einsum("hqd,hkd->hqk", head_d, head_v, preferred_element_type=jnp.float32)
        center = jnp.sum(probs * d_probs, axis=-1, keepdims=True)
        d_scores = (probs * (d_probs - center)).astype(jnp.bfloat16)
        d_vals = jnp.einsum(
            "hqk,hqd->hkd", probs.astype(jnp.bfloat16), head_d, preferred_element_type=jnp.float32
        )
        d_q = (
            jnp.einsum("hqk,hkd->hqd", d_scores, head_k, preferred_element_type=jnp.float32)
            * factor
        )
        d_k = (
            jnp.einsum("hqk,hqd->hkd", d_scores, head_q, preferred_element_type=jnp.float32)
            * factor
        )
        return (d_q, d_k, d_vals)

    dq_items, dk_items, dv_items = lax.map(
        attend_back, (query_items, back_keys, back_values, query_segs, key_segs, log_sums, d_items)
    )
    d_query = from_items(dq_items, seq_count).reshape(row_count, model_width).astype(jnp.bfloat16)
    partial_kv = (from_items(dk_items, seq_count), from_items(dv_items, seq_count))
    own_kv = (
        lax.psum_scatter(
            partial_kv[0].astype(jnp.bfloat16), "ctx", scatter_dimension=1, tiled=True
        ).astype(jnp.float32),
        lax.psum_scatter(
            partial_kv[1].astype(jnp.bfloat16), "ctx", scatter_dimension=1, tiled=True
        ).astype(jnp.float32),
    )
    d_key = own_kv[0].reshape(row_count, model_width).astype(jnp.bfloat16)
    d_value = own_kv[1].reshape(row_count, model_width).astype(jnp.bfloat16)
    g_w_query = over_rows(rows, d_query)
    g_b_query = jnp.sum(d_query.astype(jnp.float32), axis=0)
    g_w_key = over_rows(rows, d_key)
    g_w_value = over_rows(rows, d_value)
    g_b_value = jnp.sum(d_value.astype(jnp.float32), axis=0)
    input_sum = (
        d_first + against(d_query, back[0]) + against(d_key, back[2]) + against(d_value, back[3])
    )
    grad_input = input_sum.astype(jnp.bfloat16).reshape(tokens.shape)
    grads = (
        g_w_query,
        g_b_query,
        g_w_key,
        g_w_value,
        g_b_value,
        g_w_attn,
        g_b_attn,
        d_gain_one,
        d_shift_one,
        g_w_inner,
        g_b_inner,
        g_w_outer,
        g_b_outer,
        d_gain_two,
        d_shift_two,
    )
    shares = (
        lax.psum_scatter(
            grads[0].astype(jnp.bfloat16), "wt", scatter_dimension=0, tiled=True
        ).astype(jnp.float32),
        lax.psum_scatter(
            grads[1].astype(jnp.bfloat16), "wt", scatter_dimension=0, tiled=True
        ).astype(jnp.float32),
        lax.psum_scatter(
            grads[2].astype(jnp.bfloat16), "wt", scatter_dimension=0, tiled=True
        ).astype(jnp.float32),
        lax.psum_scatter(
            grads[3].astype(jnp.bfloat16), "wt", scatter_dimension=0, tiled=True
        ).astype(jnp.float32),
        lax.psum_scatter(
            grads[4].astype(jnp.bfloat16), "wt", scatter_dimension=0, tiled=True
        ).astype(jnp.float32),
        lax.psum_scatter(
            grads[5].astype(jnp.bfloat16), "wt", scatter_dimension=0, tiled=True
        ).astype(jnp.float32),
        lax.psum_scatter(
            grads[6].astype(jnp.bfloat16), "wt", scatter_dimension=0, tiled=True
        ).astype(jnp.float32),
        lax.psum_scatter(
            grads[7].astype(jnp.bfloat16), "wt", scatter_dimension=0, tiled=True
        ).astype(jnp.float32),
        lax.psum_scatter(
            grads[8].astype(jnp.bfloat16), "wt", scatter_dimension=0, tiled=True
        ).astype(jnp.float32),
        lax.psum_scatter(
            grads[9].astype(jnp.bfloat16), "wt", scatter_dimension=0, tiled=True
        ).astype(jnp.float32),
        lax.psum_scatter(
            grads[10].astype(jnp.bfloat16), "wt", scatter_dimension=0, tiled=True
        ).astype(jnp.float32),
        lax.psum_scatter(
            grads[11].astype(jnp.bfloat16), "wt", scatter_dimension=0, tiled=True
        ).astype(jnp.float32),
        lax.psum_scatter(
            grads[12].astype(jnp.bfloat16), "wt", scatter_dimension=0, tiled=True
        ).astype(jnp.float32),
        lax.psum_scatter(
            grads[13].astype(jnp.bfloat16), "wt", scatter_dimension=0, tiled=True
        ).astype(jnp.float32),
        lax.psum_scatter(
            grads[14].astype(jnp.bfloat16), "wt", scatter_dimension=0, tiled=True
        ).astype(jnp.float32),
    )
    summed = (
        lax.psum(shares[0].astype(jnp.bfloat16), ("seq", "ctx")).astype(jnp.float32),
        lax.psum(shares[1].astype(jnp.bfloat16), ("seq", "ctx")).astype(jnp.float32),
        lax.psum(shares[2].astype(jnp.bfloat16), ("seq", "ctx")).astype(jnp.float32),
        lax.psum(shares[3].astype(jnp.bfloat16), ("seq", "ctx")).astype(jnp.float32),
        lax.psum(shares[4].astype(jnp.bfloat16), ("seq", "ctx")).astype(jnp.float32),
        lax.psum(shares[5].astype(jnp.bfloat16), ("seq", "ctx")).astype(jnp.float32),
        lax.psum(shares[6].astype(jnp.bfloat16), ("seq", "ctx")).astype(jnp.float32),
        lax.psum(shares[7].astype(jnp.bfloat16), ("seq", "ctx")).astype(jnp.float32),
        lax.psum(shares[8].astype(jnp.bfloat16), ("seq", "ctx")).astype(jnp.float32),
        lax.psum(shares[9].astype(jnp.bfloat16), ("seq", "ctx")).astype(jnp.float32),
        lax.psum(shares[10].astype(jnp.bfloat16), ("seq", "ctx")).astype(jnp.float32),
        lax.psum(shares[11].astype(jnp.bfloat16), ("seq", "ctx")).astype(jnp.float32),
        lax.psum(shares[12].astype(jnp.bfloat16), ("seq", "ctx")).astype(jnp.float32),
        lax.psum(shares[13].astype(jnp.bfloat16), ("seq", "ctx")).astype(jnp.float32),
        lax.psum(shares[14].astype(jnp.bfloat16), ("seq", "ctx")).astype(jnp.float32),
    )
    return (layer_out, grad_input) + tuple(summed)


def solution(mesh):
    in_specs = (
        P(("seq", "wt"), "ctx", None),
        P(("seq", "wt"), "ctx", None),
        P(("seq", "wt"), "ctx"),
        P(("seq", "wt"), None),
        P("wt", None),
        P("wt"),
        P("wt", None),
        P("wt", None),
        P("wt"),
        P("wt", None),
        P("wt"),
        P("wt"),
        P("wt"),
        P("wt", None),
        P("wt"),
        P("wt", None),
        P("wt"),
        P("wt"),
        P("wt"),
    )
    out_specs = (
        P(("seq", "wt"), "ctx", None),
        P(("seq", "wt"), "ctx", None),
        P("wt", None),
        P("wt"),
        P("wt", None),
        P("wt", None),
        P("wt"),
        P("wt", None),
        P("wt"),
        P("wt"),
        P("wt"),
        P("wt", None),
        P("wt"),
        P("wt", None),
        P("wt"),
        P("wt"),
        P("wt"),
    )
    return jax.shard_map(body, mesh=mesh, in_specs=in_specs, out_specs=out_specs, check_vma=False)
```

profile of v0, /device:TPU:0, one launch (start us, length us, event | category | flops | bytes accessed | tf_op | source)
XLA Modules:
  0.0 968.8 jit_solution(11220610871833606484)
XLA Ops:
  17.3 21.1 %all-reduce.20 = (bf16[768]{0:T(1024)(128)(2,1)S(1)}, bf16[768]{0:T(1024)(128)(2,1)S(1)}, bf16[768]{0:T(1024)(128)(2,1)S(1)}, bf16[768]{0:T(1024)(128)(2,1)S(1)}...) all-reduce(bf16[768]{0:T(1024)(128)(2,1)S(1)} %dynamic-update-slice, ...), channel_id=1, replica_groups=mesh['seq'=2,'ctx'=4,'wt'=4] {'wt'}, use_global_device_ids=true, to_apply=%add | all-reduce | flops 5376 | bytes 21504
  38.4 4.9 all-gather.16.cloned.1.call-done
  46.9 27.5 %all-gather.12.cloned.1.call-done = bf16[768,768]{1,0:T(8,128)(2,1)} async-done(((bf16[192,768]{1,0:T(8,128)(2,1)}), bf16[768,768]{1,0:T(8,128)(2,1)}) %all-gather.12.cloned.1.call-update) | async-done | bytes 1179664 | tf_op jit(solution)/shard_map/all_gather | solution.py:114
  81.1 13.6 %all-gather = bf16[4,1,768]{2,1,0:T(2,128)(2,1)S(1)} all-gather(bf16[1,1,768]{2,1,0:T(2,128)(2,1)S(1)} %reshape.309), channel_id=1, replica_groups=mesh['seq'=2,'ctx'=4,'wt'=4] {'wt'}, dimensions={0}, use_global_device_ids=true | all-gather | bytes 7680 | tf_op jit(solution)/shard_map/all_gather | solution.py:122
  94.7 11.1 %all-gather.10.cloned.1.call-done = bf16[768,768]{1,0:T(8,128)(2,1)} async-done(((bf16[192,768]{1,0:T(8,128)(2,1)}), bf16[768,768]{1,0:T(8,128)(2,1)}) %all-gather.10.cloned.1.call-update) | async-done | bytes 1179664 | tf_op jit(solution)/shard_map/all_gather | solution.py:112
  108.5 27.4 %all-gather.18.cloned.1.call-done = bf16[2,1024,768]{1,2,0:T(8,128)(2,1)} async-done(((bf16[2,256,768]{1,2,0:T(8,128)(2,1)}), bf16[2,1024,768]{1,2,0:T(8,128)(2,1)}) %all-gather.18.cloned.1.call-update) | async-done | bytes 3145744 | tf_op jit(solution)/shard_map/all_gather | solution.py:138
  135.8 30.9 %all-gather.14.cloned.1.call-done = bf16[2,1024,768]{1,2,0:T(8,128)(2,1)} async-done(((bf16[2,256,768]{1,2,0:T(8,128)(2,1)}), bf16[2,1024,768]{1,2,0:T(8,128)(2,1)}) %all-gather.14.cloned.1.call-update) | async-done | bytes 3145744 | tf_op jit(solution)/shard_map/all_gather | solution.py:137
  166.9 34.3 %while.26 = (s32[]{:T(128)}, bf16[6,4,256,64]{2,3,1,0:T(8,128)(2,1)S(1)}, f32[6,4,256]{2,1,0:T(4,128)S(1)}, s32[6,256]{1,0:T(8,128)S(1)}, s32[6,1024]{1,0:T(8,12...) while((s32[]{:T(128)}, ...), condition=%wide.region_5.6_spmd, body=%wide.region_2.5_spmd.sunk | while | flops 280230912 | bytes 15123561 | solution.py:157
  205.2 83.6 %all-gather.22.cloned.1.call-done = bf16[768,3072]{1,0:T(8,128)(2,1)} async-done(((bf16[192,3072]{1,0:T(8,128)(2,1)}), bf16[768,3072]{1,0:T(8,128)(2,1)}) %all-gather.22.cloned.1.call-update) | async-done | bytes 4718608 | tf_op jit(solution)/shard_map/all_gather | solution.py:121
  288.8 19.8 %multiply_convert_fusion.1 = (bf16[512,3072]{1,0:T(8,128)(2,1)}, f32[512,3072]{1,0:T(8,128)}, f32[512,3072]{1,0:T(8,128)}) fusion(f32[3072]{0:T(1024)S(1)} %bitcast.251, bf16[768,3072]{1,0:T(8,128)(2,1)} %all-gather.22.cloned.1.call-done, f32[512,768]{1,0:T(8,128)S(1)} %get-tuple-element.307, f32[768]{0:T(1024)S(1)} %convert_element_type.289, ...), kind=kOutput, calls=%fused_computation.68 | convolution fusion | flops 2521694208 | bytes 22042624 | tf_op jit(solution)/shard_map/dot_general | solution.py:14
  308.6 69.7 %all-gather.24.cloned.1.call-done = bf16[3072,768]{1,0:T(8,128)(2,1)} async-done(((bf16[768,768]{1,0:T(8,128)(2,1)}), bf16[3072,768]{1,0:T(8,128)(2,1)}) %all-gather.24.cloned.1.call-update) | async-done | bytes 4718608 | tf_op jit(solution)/shard_map/all_gather | solution.py:123
  378.3 6.1 fusion.78
  388.1 7.9 fusion.71
  396.1 3.1 multiply_reduce_fusion.3
  412.5 83.7 %while.27 = (s32[]{:T(128)}, bf16[6,4,256,64]{2,3,1,0:T(8,128)(2,1)}, bf16[6,4,1024,64]{2,3,1,0:T(8,128)(2,1)}, bf16[6,4,1024,64]{2,3,1,0:T(8,128)(2,1)}, s32[6,...) while((s32[]{:T(128)}, ...), condition=%wide.region_16.17_spmd, body=%wide.region_14.16_spmd.sunk | while | flops 687406080 | bytes 37011584 | solution.py:235
  504.4 28.4 %reduce-scatter.17.cloned.1.call-done = bf16[2,256,768]{1,2,0:T(8,128)(2,1)} async-done(((bf16[2,1024,768]{1,2,0:T(8,128)(2,1)}), bf16[2,256,768]{1,2,0:T(8,128)(2,1)}) %reduce-scatter.17.cloned.1.call-update) | async-done | bytes 786448 | tf_op jit(solution)/shard_map/reduce_scatter | solution.py:244
  532.8 3.2 fusion.62
  538.4 34.9 %reduce-scatter.15.cloned.1.call-done = bf16[2,256,768]{1,2,0:T(8,128)(2,1)} async-done(((bf16[2,1024,768]{1,2,0:T(8,128)(2,1)}), bf16[2,256,768]{1,2,0:T(8,128)(2,1)}) %reduce-scatter.15.cloned.1.call-update) | async-done | bytes 786448 | tf_op jit(solution)/shard_map/reduce_scatter | solution.py:241
  573.3 3.2 fusion.61
  578.9 3.2 convolution_convert_fusion.2
  582.3 7.4 convolution_convert_fusion.1
  589.7 6.9 convolution_convert_fusion
  598.3 6.5 reduce-scatter.25.cloned.1.call-done
  606.7 28.2 %reduce-scatter.29.cloned.1.call-done = bf16[192,768]{1,0:T(8,128)(2,1)} async-done(((bf16[768,768]{1,0:T(8,128)(2,1)}), bf16[192,768]{1,0:T(8,128)(2,1)}) %reduce-scatter.29.cloned.1.call-update) | async-done | bytes 294928
  636.8 28.4 %reduce-scatter.27.cloned.1.call-done = bf16[192,768]{1,0:T(8,128)(2,1)} async-done(((bf16[768,768]{1,0:T(8,128)(2,1)}), bf16[192,768]{1,0:T(8,128)(2,1)}) %reduce-scatter.27.cloned.1.call-update) | async-done | bytes 294928
  667.0 28.8 %reduce-scatter.19.cloned.1.call-done = bf16[192,768]{1,0:T(8,128)(2,1)} async-done(((bf16[768,768]{1,0:T(8,128)(2,1)}), bf16[192,768]{1,0:T(8,128)(2,1)}) %reduce-scatter.19.cloned.1.call-update) | async-done | bytes 294928 | tf_op jit(solution)/shard_map/reduce_scatter | solution.py:292
  695.8 86.2 %reduce-scatter.21.cloned.1.call-done = bf16[192,3072]{1,0:T(8,128)(2,1)} async-done(((bf16[768,3072]{1,0:T(8,128)(2,1)}), bf16[192,3072]{1,0:T(8,128)(2,1)}) %reduce-scatter.21.cloned.1.call-update) | async-done | bytes 1179664 | tf_op jit(solution)/shard_map/reduce_scatter | solution.py:304
  782.0 88.0 %reduce-scatter.23.cloned.1.call-done = bf16[768,768]{1,0:T(8,128)(2,1)} async-done(((bf16[3072,768]{1,0:T(8,128)(2,1)}), bf16[768,768]{1,0:T(8,128)(2,1)}) %reduce-scatter.23.cloned.1.call-update) | async-done | bytes 1179664 | tf_op jit(solution)/shard_map/reduce_scatter | solution.py:310
  874.5 3.5 fusion.79
  879.3 18.2 %all-reduce.19 = (bf16[768]{0:T(1024)(128)(2,1)S(1)}, bf16[768]{0:T(1024)(128)(2,1)S(1)}, bf16[768]{0:T(1024)(128)(2,1)S(1)}, bf16[768]{0:T(1024)(128)(2,1)S(1)}...) all-reduce(bf16[768]{0:T(1024)(128)(2,1)S(1)} %dynamic-update-slice, ...), channel_id=1, replica_groups=mesh['seq'=2,'ctx'=4,'wt'=4] {'wt'}, use_global_device_ids=true, to_apply=%add.7 | all-reduce | flops 9984 | bytes 39936
  898.2 12.5 %all-reduce.17 = (bf16[192]{0:T(256)(128)(2,1)S(1)}, bf16[192]{0:T(256)(128)(2,1)S(1)}, bf16[192]{0:T(256)(128)(2,1)S(1)}, bf16[192]{0:T(256)(128)(2,1)S(1)}, bf...) all-reduce(bf16[192]{0:T(256)(128)(2,1)S(1)} %dynamic-slice.9, ...), channel_id=1, replica_groups=mesh['seq'=2,'ctx'=4,'wt'=4] {'seq','ctx'}, use_global_device_ids=true, to_apply=%region_23.24 | all-reduce | flops 2304 | bytes 9216 | tf_op jit(solution)/shard_map/psum | solution.py:325
  926.0 27.6 %all-reduce.23.cloned.1.call-done = (bf16[192,768]{0,1:T(8,128)(2,1)}, bf16[192,768]{0,1:T(8,128)(2,1)}, bf16[192,768]{0,1:T(8,128)(2,1)}, bf16[192,768]{1,0:T(8...) async-done(((bf16[192,768]{0,1:T(8,128)(2,1)}, bf16[192,768]{0,1:T(8,128)(2,1)}, bf16[192,768]{0,1:T(8,128)(2,1)}, bf16[192,768]{1,0:T(8,128)(2,1)}, ...) | async-done | bytes 3538960 | tf_op jit(solution)/shard_map/psum | solution.py:324
  (306 shorter events, 209.6 us)
Async XLA Ops:
  7.2 36.1 %all-gather.16.cloned.1.call-start = ((), (), s32[]{:S(2)}) async-start(), calls=%async_computation.11 | async-start | bytes 1474560 | tf_op jit(solution)/shard_map/all_gather | solution.py:115
  7.9 66.5 %all-gather.12.cloned.1.call-start = ((), (), s32[]{:S(2)}) async-start(), calls=%async_computation.9 | async-start | bytes 1474560 | tf_op jit(solution)/shard_map/all_gather | solution.py:114
  8.7 97.1 %all-gather.10.cloned.1.call-start = ((), (), s32[]{:S(2)}) async-start(), calls=%async_computation.8 | async-start | bytes 1474560 | tf_op jit(solution)/shard_map/all_gather | solution.py:112
  9.4 126.4 %all-gather.18.cloned.1.call-start = ((), (), s32[]{:S(2)}) async-start(), calls=%async_computation.12 | async-start | bytes 3932160 | tf_op jit(solution)/shard_map/all_gather | solution.py:138
  43.3 31.1 %copy-start.21 = (bf16[2,256,768]{2,1,0:T(8,128)(2,1)S(1)}, bf16[2,256,768]{2,1,0:T(8,128)(2,1)}, u32[]{:S(2)}) copy-start(bf16[2,256,768]{2,1,0:T(8,128)(2,1)} %param.23) | copy-start | bytes 2359300
  46.9 119.9 %all-gather.14.cloned.1.call-start = ((), (), s32[]{:S(2)}) async-start(), calls=%async_computation.10 | async-start | bytes 3932160 | tf_op jit(solution)/shard_map/all_gather | solution.py:137
  76.5 3.9 copy-start.16
  76.5 4.6 copy-start.17
  77.7 124.5 %all-gather.20.cloned.1.call-start = ((), (), s32[]{:S(2)}) async-start(), calls=%async_computation.13 | async-start | bytes 1474560 | tf_op jit(solution)/shard_map/all_gather | solution.py:117
  78.3 210.5 %all-gather.22.cloned.1.call-start = ((), (), s32[]{:S(2)}) async-start(), calls=%async_computation.14 | async-start | bytes 5898240 | tf_op jit(solution)/shard_map/all_gather | solution.py:121
  79.1 299.3 %all-gather.24.cloned.1.call-start = ((), (), s32[]{:S(2)}) async-start(), calls=%async_computation.15 | async-start | bytes 5898240 | tf_op jit(solution)/shard_map/all_gather | solution.py:123
  79.8 453.0 %reduce-scatter.17.cloned.1.call-start = ((), (), s32[]{:S(2)}) async-start(), calls=%async_computation.17 | async-start | bytes 3932160 | tf_op jit(solution)/shard_map/reduce_scatter | solution.py:244
  204.9 191.1 %copy-start.2 = (f32[512,768]{1,0:T(8,128)}, f32[512,768]{1,0:T(8,128)S(1)}, u32[]{:S(2)}) copy-start(f32[512,768]{1,0:T(8,128)S(1)} %get-tuple-element.307) | copy-start | bytes 4718596
  378.3 6.4 copy-start.1
  386.2 9.8 %slice-start = ((s8[4718592]{0:T(1024)(128)(4,1)}), s8[4194304]{0:T(1024)(128)(4,1)S(1)}, s32[]{:S(2)}) async-start(s8[4718592]{0:T(1024)(128)(4,1)} %bitcast.253), calls=%async_computation.25 | async-start | bytes 8388608
  386.4 9.6 copy-start.9
  388.1 8.0 slice-start.1
  496.2 77.0 %reduce-scatter.15.cloned.1.call-start = ((), (), s32[]{:S(2)}) async-start(), calls=%async_computation.16 | async-start | bytes 3932160 | tf_op jit(solution)/shard_map/reduce_scatter | solution.py:241
  496.8 108.0 %reduce-scatter.25.cloned.1.call-start = ((), (), s32[]{:S(2)}) async-start(), calls=%async_computation.21 | async-start | bytes 1474560
  504.3 130.6 %reduce-scatter.29.cloned.1.call-start = ((), (), s32[]{:S(2)}) async-start(), calls=%async_computation.23 | async-start | bytes 1474560
  538.3 126.8 %reduce-scatter.27.cloned.1.call-start = ((), (), s32[]{:S(2)}) async-start(), calls=%async_computation.22 | async-start | bytes 1474560
  578.8 117.0 %reduce-scatter.19.cloned.1.call-start = ((), (), s32[]{:S(2)}) async-start(), calls=%async_computation.18 | async-start | bytes 1474560 | tf_op jit(solution)/shard_map/reduce_scatter | solution.py:292
  582.1 199.9 %reduce-scatter.21.cloned.1.call-start = ((), (), s32[]{:S(2)}) async-start(), calls=%async_computation.19 | async-start | bytes 5898240 | tf_op jit(solution)/shard_map/reduce_scatter | solution.py:304
  589.7 280.3 %reduce-scatter.23.cloned.1.call-start = ((), (), s32[]{:S(2)}) async-start(), calls=%async_computation.20 | async-start | bytes 5898240 | tf_op jit(solution)/shard_map/reduce_scatter | solution.py:310
  596.7 273.3 %copy-start.15 = (f32[2,256]{1,0:T(2,128)S(1)}, f32[2,256]{1,0:T(2,128)}, u32[]{:S(2)}) copy-start(f32[2,256]{1,0:T(2,128)} %get-tuple-element.302) | copy-start | bytes 6148
  596.7 356.9 %all-reduce.23.cloned.1.call-start = ((), (), s32[]{:S(2)}) async-start(), calls=%async_computation.24 | async-start | bytes 7667712 | tf_op jit(solution)/shard_map/psum | solution.py:324
  920.3 3.9 copy-start.3
  920.3 3.9 copy-start.4
  920.4 3.9 copy-start.6
  953.6 4.7 copy-start.14
  953.6 5.5 copy-start.13
  956.7 4.4 copy-start.11
  (12 other events, 32.0 us)
Sparse Core Ops, SparseCore 0:
  9.6 33.6 all-gather.15
  44.9 29.5 all-gather.11
  76.0 29.7 all-gather.9
  107.8 28.0 all-gather.17
  137.8 28.9 all-gather.13
  168.2 30.4 all-gather.19
  200.3 88.5 all-gather.21
  290.4 87.8 all-gather.23
  496.3 36.3 reduce-scatter.16
  535.3 37.9 reduce-scatter.14
  575.6 29.1 reduce-scatter.24
  607.0 27.8 reduce-scatter.28
  637.2 27.8 reduce-scatter.26
  667.9 27.8 reduce-scatter.18
  698.0 83.9 reduce-scatter.20
  784.1 85.7 reduce-scatter.22
  874.5 79.0 all-reduce.22
where the time goes:
time: 975 us; the launch traced here: 969 us
  waiting for transfers between devices  617 us (63%)
  matrix products  181 us (19%)
  blocking collectives  65.3 us (7%)
  local copies, waits for them, and re-layouts  47.2 us (5%)
  other arithmetic  40.5 us (4%)
  between operations  16.7 us (2%)
    reduce_scatter x1, waiting for transfers between devices, body(): lax.psum_scatter(grads[11].astype(jnp.bfloat16), 'wt', scatter_dimension=...  88 us
    reduce_scatter x1, waiting for transfers between devices, body(): lax.psum_scatter(grads[9].astype(jnp.bfloat16), 'wt', scatter_dimension=0...  86.2 us
    all_gather x1, waiting for transfers between devices, body(): lax.all_gather(shards[9], 'wt', axis=0, tiled=True)  83.6 us
    all_gather x1, waiting for transfers between devices, body(): lax.all_gather(shards[11], 'wt', axis=0, tiled=True)  69.7 us
    unnamed x20, waiting for transfers between devices  67.8 us
    unnamed x2, blocking collectives  39.3 us
    dot_general x6, matrix products, product(): return jnp.dot(former, latter, preferred_element_type=jnp.float32)  35 us
    reduce_scatter x1, waiting for transfers between devices, body(): lax.psum_scatter(partial_kv[0].astype(jnp.bfloat16), 'ctx', scatter_dimen...  34.9 us
  transfers between devices with their start and end apart: 17, of which 16 were waited for; matrix products, arithmetic and copies ran while one was open for 15% of the time, Pallas kernels for 0%

commit v1 on v0

--- a/solution.py
+++ b/solution.py
@@ -8,6 +8,12 @@
 HD = 64
 NEG = -1000000000.0
 EPS = 1e-05
+
+
+def name_loads_over_axis(patch, net_axis, bus_axis):
+    for dd in (net_axis, bus_axis):
+        patch = lax.psum(patch, dd)
+    return patch
 
 
 def product(former, latter):
@@ -321,7 +327,7 @@
         ).astype(jnp.float32),
     )
     summed = (
-        lax.psum(shares[0].astype(jnp.bfloat16), ("seq", "ctx")).astype(jnp.float32),
+        name_loads_over_axis(shares[0].astype(jnp.bfloat16), "ctx", "seq").astype(jnp.float32),
         lax.psum(shares[1].astype(jnp.bfloat16), ("seq", "ctx")).astype(jnp.float32),
         lax.psum(shares[2].astype(jnp.bfloat16), ("seq", "ctx")).astype(jnp.float32),
         lax.psum(shares[3].astype(jnp.bfloat16), ("seq", "ctx")).astype(jnp.float32),

time: 975 us -> 1040 us (1.067)
  waiting for transfers between devices: 617 us -> 681 us
    psum x1 -> x3, waiting for transfers between devices: 27.6 us -> 58.9 us  [the longest x2 30.9 us: name_loads_over_axis(): patch = lax.psum(patch, dd)]
    unnamed x20 -> x22, waiting for transfers between devices: 67.8 us -> 91.7 us
    unnamed x93 -> x91, local copies, waits for them, and re-layouts: 27.9 us -> 28.7 us
  transfers between devices with their start and end apart: 17 -> 19, of which waited for: 16 -> 18; matrix products, arithmetic and copies ran while one was open for 15% -> 13% of each run, Pallas kernels for 0% -> 0%
where the time goes in v1:
time: 1040 us; the launch traced here: 1030 us
  waiting for transfers between devices  681 us (65%)
  matrix products  181 us (17%)
  blocking collectives  66 us (6%)
  local copies, waits for them, and re-layouts  48 us (5%)
  other arithmetic  40.5 us (4%)
  between operations  16.8 us (2%)
    unnamed x22, waiting for transfers between devices  91.7 us
    reduce_scatter x1, waiting for transfers between devices, body(): lax.psum_scatter(grads[11].astype(jnp.bfloat16), 'wt', scatter_dimension=...  88.1 us
    reduce_scatter x1, waiting for transfers between devices, body(): lax.psum_scatter(grads[9].astype(jnp.bfloat16), 'wt', scatter_dimension=0...  86.3 us
    all_gather x1, waiting for transfers between devices, body(): lax.all_gather(shards[9], 'wt', axis=0, tiled=True)  83.6 us
    all_gather x1, waiting for transfers between devices, body(): lax.all_gather(shards[11], 'wt', axis=0, tiled=True)  69.7 us
    unnamed x2, blocking collectives  40 us
    reduce_scatter x1, waiting for transfers between devices, body(): lax.psum_scatter(partial_kv[1].astype(jnp.bfloat16), 'ctx', scatter_dimen...  37.1 us
    reduce_scatter x1, waiting for transfers between devices, body(): lax.psum_scatter(partial_kv[0].astype(jnp.bfloat16), 'ctx', scatter_dimen...  35.1 us
  transfers between devices with their start and end apart: 19, of which 18 were waited for; matrix products, arithmetic and copies ran while one was open for 13% of the time, Pallas kernels for 0%

profile of v1, /device:TPU:0, one launch (start us, length us, event | category | flops | bytes accessed | tf_op | source)
XLA Modules:
  0.0 1034.9 jit_solution(3702302328689434122)
XLA Ops:
  17.3 21.1 %all-reduce.20 = (bf16[768]{0:T(1024)(128)(2,1)S(1)}, bf16[768]{0:T(1024)(128)(2,1)S(1)}, bf16[768]{0:T(1024)(128)(2,1)S(1)}, bf16[768]{0:T(1024)(128)(2,1)S(1)}...) all-reduce(bf16[768]{0:T(1024)(128)(2,1)S(1)} %dynamic-update-slice, ...), channel_id=1, replica_groups=mesh['seq'=2,'ctx'=4,'wt'=4] {'wt'}, use_global_device_ids=true, to_apply=%add | all-reduce | flops 5376 | bytes 21504
  38.4 4.9 all-gather.16.cloned.1.call-done
  46.9 27.5 %all-gather.12.cloned.1.call-done = bf16[768,768]{1,0:T(8,128)(2,1)} async-done(((bf16[192,768]{1,0:T(8,128)(2,1)}), bf16[768,768]{1,0:T(8,128)(2,1)}) %all-gather.12.cloned.1.call-update) | async-done | bytes 1179664 | tf_op jit(solution)/shard_map/all_gather | solution.py:120
  81.1 13.6 %all-gather = bf16[4,1,768]{2,1,0:T(2,128)(2,1)S(1)} all-gather(bf16[1,1,768]{2,1,0:T(2,128)(2,1)S(1)} %reshape.309), channel_id=1, replica_groups=mesh['seq'=2,'ctx'=4,'wt'=4] {'wt'}, dimensions={0}, use_global_device_ids=true | all-gather | bytes 7680 | tf_op jit(solution)/shard_map/all_gather | solution.py:128
  94.7 11.1 %all-gather.10.cloned.1.call-done = bf16[768,768]{1,0:T(8,128)(2,1)} async-done(((bf16[192,768]{1,0:T(8,128)(2,1)}), bf16[768,768]{1,0:T(8,128)(2,1)}) %all-gather.10.cloned.1.call-update) | async-done | bytes 1179664 | tf_op jit(solution)/shard_map/all_gather | solution.py:118
  108.5 27.4 %all-gather.18.cloned.1.call-done = bf16[2,1024,768]{1,2,0:T(8,128)(2,1)} async-done(((bf16[2,256,768]{1,2,0:T(8,128)(2,1)}), bf16[2,1024,768]{1,2,0:T(8,128)(2,1)}) %all-gather.18.cloned.1.call-update) | async-done | bytes 3145744 | tf_op jit(solution)/shard_map/all_gather | solution.py:144
  135.8 30.9 %all-gather.14.cloned.1.call-done = bf16[2,1024,768]{1,2,0:T(8,128)(2,1)} async-done(((bf16[2,256,768]{1,2,0:T(8,128)(2,1)}), bf16[2,1024,768]{1,2,0:T(8,128)(2,1)}) %all-gather.14.cloned.1.call-update) | async-done | bytes 3145744 | tf_op jit(solution)/shard_map/all_gather | solution.py:143
  166.9 34.3 %while.26 = (s32[]{:T(128)}, bf16[6,4,256,64]{2,3,1,0:T(8,128)(2,1)S(1)}, f32[6,4,256]{2,1,0:T(4,128)S(1)}, s32[6,256]{1,0:T(8,128)S(1)}, s32[6,1024]{1,0:T(8,12...) while((s32[]{:T(128)}, ...), condition=%wide.region_5.6_spmd, body=%wide.region_2.5_spmd.sunk | while | flops 280230912 | bytes 15123561 | solution.py:163
  205.2 83.6 %all-gather.22.cloned.1.call-done = bf16[768,3072]{1,0:T(8,128)(2,1)} async-done(((bf16[192,3072]{1,0:T(8,128)(2,1)}), bf16[768,3072]{1,0:T(8,128)(2,1)}) %all-gather.22.cloned.1.call-update) | async-done | bytes 4718608 | tf_op jit(solution)/shard_map/all_gather | solution.py:127
  288.8 19.8 %multiply_convert_fusion.1 = (bf16[512,3072]{1,0:T(8,128)(2,1)}, f32[512,3072]{1,0:T(8,128)}, f32[512,3072]{1,0:T(8,128)}) fusion(f32[3072]{0:T(1024)S(1)} %bitcast.251, bf16[768,3072]{1,0:T(8,128)(2,1)} %all-gather.22.cloned.1.call-done, f32[512,768]{1,0:T(8,128)S(1)} %get-tuple-element.306, f32[768]{0:T(1024)S(1)} %convert_element_type.289, ...), kind=kOutput, calls=%fused_computation.68 | convolution fusion | flops 2521694208 | bytes 22042624 | tf_op jit(solution)/shard_map/dot_general | solution.py:20
  308.6 69.7 %all-gather.24.cloned.1.call-done = bf16[3072,768]{1,0:T(8,128)(2,1)} async-done(((bf16[768,768]{1,0:T(8,128)(2,1)}), bf16[3072,768]{1,0:T(8,128)(2,1)}) %all-gather.24.cloned.1.call-update) | async-done | bytes 4718608 | tf_op jit(solution)/shard_map/all_gather | solution.py:129
  378.3 6.1 fusion.78
  388.1 7.9 fusion.71
  412.5 83.7 %while.27 = (s32[]{:T(128)}, bf16[6,4,256,64]{2,3,1,0:T(8,128)(2,1)}, bf16[6,4,1024,64]{2,3,1,0:T(8,128)(2,1)}, bf16[6,4,1024,64]{2,3,1,0:T(8,128)(2,1)}, s32[6,...) while((s32[]{:T(128)}, ...), condition=%wide.region_16.17_spmd, body=%wide.region_14.16_spmd.sunk | while | flops 687406080 | bytes 37011584 | solution.py:241
  504.8 26.4 %reduce-scatter.25.cloned.1.call-done = bf16[192,768]{1,0:T(8,128)(2,1)} async-done(((bf16[768,768]{1,0:T(8,128)(2,1)}), bf16[192,768]{1,0:T(8,128)(2,1)}) %reduce-scatter.25.cloned.1.call-update) | async-done | bytes 294928
  533.2 37.1 %reduce-scatter.17.cloned.1.call-done = bf16[2,256,768]{1,2,0:T(8,128)(2,1)} async-done(((bf16[2,1024,768]{1,2,0:T(8,128)(2,1)}), bf16[2,256,768]{1,2,0:T(8,128)(2,1)}) %reduce-scatter.17.cloned.1.call-update) | async-done | bytes 786448 | tf_op jit(solution)/shard_map/reduce_scatter | solution.py:250
  570.3 3.2 fusion.62
  575.9 35.1 %reduce-scatter.15.cloned.1.call-done = bf16[2,256,768]{1,2,0:T(8,128)(2,1)} async-done(((bf16[2,1024,768]{1,2,0:T(8,128)(2,1)}), bf16[2,256,768]{1,2,0:T(8,128)(2,1)}) %reduce-scatter.15.cloned.1.call-update) | async-done | bytes 786448 | tf_op jit(solution)/shard_map/reduce_scatter | solution.py:247
  616.6 3.2 convolution_convert_fusion.2
  620.0 7.4 convolution_convert_fusion.1
  627.4 6.9 convolution_convert_fusion
  634.5 11.9 %all-reduce.25.cloned.1.call-done = bf16[192,768]{0,1:T(8,128)(2,1)} async-done(((bf16[192,768]{0,1:T(8,128)(2,1)}), bf16[192,768]{0,1:T(8,128)(2,1)}) %all-reduce.25.cloned.1.call-update) | async-done | bytes 294928 | tf_op jit(solution)/shard_map/psum | solution.py:15
  646.5 31.6 %reduce-scatter.29.cloned.1.call-done = bf16[192,768]{1,0:T(8,128)(2,1)} async-done(((bf16[768,768]{1,0:T(8,128)(2,1)}), bf16[192,768]{1,0:T(8,128)(2,1)}) %reduce-scatter.29.cloned.1.call-update) | async-done | bytes 294928
  679.9 28.3 %reduce-scatter.27.cloned.1.call-done = bf16[192,768]{1,0:T(8,128)(2,1)} async-done(((bf16[768,768]{1,0:T(8,128)(2,1)}), bf16[192,768]{1,0:T(8,128)(2,1)}) %reduce-scatter.27.cloned.1.call-update) | async-done | bytes 294928
  710.1 28.9 %reduce-scatter.19.cloned.1.call-done = bf16[192,768]{1,0:T(8,128)(2,1)} async-done(((bf16[768,768]{1,0:T(8,128)(2,1)}), bf16[192,768]{1,0:T(8,128)(2,1)}) %reduce-scatter.19.cloned.1.call-update) | async-done | bytes 294928 | tf_op jit(solution)/shard_map/reduce_scatter | solution.py:298
  739.0 86.3 %reduce-scatter.21.cloned.1.call-done = bf16[192,3072]{1,0:T(8,128)(2,1)} async-done(((bf16[768,3072]{1,0:T(8,128)(2,1)}), bf16[192,3072]{1,0:T(8,128)(2,1)}) %reduce-scatter.21.cloned.1.call-update) | async-done | bytes 1179664 | tf_op jit(solution)/shard_map/reduce_scatter | solution.py:310
  825.3 88.1 %reduce-scatter.23.cloned.1.call-done = bf16[768,768]{1,0:T(8,128)(2,1)} async-done(((bf16[3072,768]{1,0:T(8,128)(2,1)}), bf16[768,768]{1,0:T(8,128)(2,1)}) %reduce-scatter.23.cloned.1.call-update) | async-done | bytes 1179664 | tf_op jit(solution)/shard_map/reduce_scatter | solution.py:316
  919.4 3.5 fusion.79
  922.9 18.9 %all-reduce.27.cloned.1.call-done = bf16[192,768]{0,1:T(8,128)(2,1)} async-done(((bf16[192,768]{0,1:T(8,128)(2,1)}), bf16[192,768]{0,1:T(8,128)(2,1)}) %all-reduce.27.cloned.1.call-update) | async-done | bytes 294928 | tf_op jit(solution)/shard_map/psum | solution.py:15
  945.2 19.0 %all-reduce.19 = (bf16[768]{0:T(1024)(128)(2,1)S(1)}, bf16[768]{0:T(1024)(128)(2,1)S(1)}, bf16[768]{0:T(1024)(128)(2,1)S(1)}, bf16[768]{0:T(1024)(128)(2,1)S(1)}...) all-reduce(bf16[768]{0:T(1024)(128)(2,1)S(1)} %dynamic-update-slice, ...), channel_id=1, replica_groups=mesh['seq'=2,'ctx'=4,'wt'=4] {'wt'}, use_global_device_ids=true, to_apply=%add.7 | all-reduce | flops 9984 | bytes 39936
  964.8 12.4 %all-reduce.17 = (bf16[192]{0:T(256)(128)(2,1)S(1)}, bf16[192]{0:T(256)(128)(2,1)S(1)}, bf16[192]{0:T(256)(128)(2,1)S(1)}, bf16[192]{0:T(256)(128)(2,1)S(1)}, bf...) all-reduce(bf16[192]{0:T(256)(128)(2,1)S(1)} %dynamic-slice.9, ...), channel_id=1, replica_groups=mesh['seq'=2,'ctx'=4,'wt'=4] {'seq','ctx'}, use_global_device_ids=true, to_apply=%region_24.25 | all-reduce | flops 2304 | bytes 9216 | tf_op jit(solution)/shard_map/psum | solution.py:331
  992.6 28.0 %all-reduce.29.cloned.1.call-done = (bf16[192,768]{0,1:T(8,128)(2,1)}, bf16[192,768]{0,1:T(8,128)(2,1)}, bf16[192,768]{1,0:T(8,128)(2,1)}, bf16[192,3072]{1,0:T(8,128)(2,1)}, bf16[768,768]{1,0:T(8,128)(2,1)}) async-done(((bf16[192,768]{0,1:T(8,128)(2,1)}, bf16[192,768]{0,1:T(8,128)(2,1)}, bf16[192,768]{1,0:T(8,128)(2,1)}, bf16[192,3072]{1,0:T(8,128)(2,1)}, bf16[768,768]{1,0:T(8,128)(2,1)}), ...) | async-done | bytes 3244048 | tf_op jit(solution)/shard_map/psum | solution.py:332
  (310 shorter events, 217.5 us)
Async XLA Ops:
  7.2 36.1 %all-gather.16.cloned.1.call-start = ((), (), s32[]{:S(2)}) async-start(), calls=%async_computation.11 | async-start | bytes 1474560 | tf_op jit(solution)/shard_map/all_gather | solution.py:121
  7.9 66.5 %all-gather.12.cloned.1.call-start = ((), (), s32[]{:S(2)}) async-start(), calls=%async_computation.9 | async-start | bytes 1474560 | tf_op jit(solution)/shard_map/all_gather | solution.py:120
  8.7 97.1 %all-gather.10.cloned.1.call-start = ((), (), s32[]{:S(2)}) async-start(), calls=%async_computation.8 | async-start | bytes 1474560 | tf_op jit(solution)/shard_map/all_gather | solution.py:118
  9.4 126.4 %all-gather.18.cloned.1.call-start = ((), (), s32[]{:S(2)}) async-start(), calls=%async_computation.12 | async-start | bytes 3932160 | tf_op jit(solution)/shard_map/all_gather | solution.py:144
  43.3 31.1 %copy-start.20 = (bf16[2,256,768]{2,1,0:T(8,128)(2,1)S(1)}, bf16[2,256,768]{2,1,0:T(8,128)(2,1)}, u32[]{:S(2)}) copy-start(bf16[2,256,768]{2,1,0:T(8,128)(2,1)} %param.23) | copy-start | bytes 2359300
  46.9 119.9 %all-gather.14.cloned.1.call-start = ((), (), s32[]{:S(2)}) async-start(), calls=%async_computation.10 | async-start | bytes 3932160 | tf_op jit(solution)/shard_map/all_gather | solution.py:143
  76.5 3.9 copy-start.15
  76.5 4.6 copy-start.16
  77.7 124.5 %all-gather.20.cloned.1.call-start = ((), (), s32[]{:S(2)}) async-start(), calls=%async_computation.13 | async-start | bytes 1474560 | tf_op jit(solution)/shard_map/all_gather | solution.py:123
  78.3 210.5 %all-gather.22.cloned.1.call-start = ((), (), s32[]{:S(2)}) async-start(), calls=%async_computation.14 | async-start | bytes 5898240 | tf_op jit(solution)/shard_map/all_gather | solution.py:127
  79.1 299.3 %all-gather.24.cloned.1.call-start = ((), (), s32[]{:S(2)}) async-start(), calls=%async_computation.15 | async-start | bytes 5898240 | tf_op jit(solution)/shard_map/all_gather | solution.py:129
  79.8 451.4 %reduce-scatter.25.cloned.1.call-start = ((), (), s32[]{:S(2)}) async-start(), calls=%async_computation.23 | async-start | bytes 1474560
  204.9 191.1 %copy-start.2 = (f32[512,768]{1,0:T(8,128)}, f32[512,768]{1,0:T(8,128)S(1)}, u32[]{:S(2)}) copy-start(f32[512,768]{1,0:T(8,128)S(1)} %get-tuple-element.306) | copy-start | bytes 4718596
  378.3 6.4 copy-start.1
  386.2 9.8 slice-start
  386.4 9.6 copy-start.9
  388.1 7.9 slice-start.1
  503.4 66.9 %reduce-scatter.17.cloned.1.call-start = ((), (), s32[]{:S(2)}) async-start(), calls=%async_computation.17 | async-start | bytes 3932160 | tf_op jit(solution)/shard_map/reduce_scatter | solution.py:250
  504.0 106.9 %reduce-scatter.15.cloned.1.call-start = ((), (), s32[]{:S(2)}) async-start(), calls=%async_computation.16 | async-start | bytes 3932160 | tf_op jit(solution)/shard_map/reduce_scatter | solution.py:247
  504.8 141.7 %all-reduce.25.cloned.1.call-start = ((), (), s32[]{:S(2)}) async-start(), calls=%async_computation.18 | async-start | bytes 786432 | tf_op jit(solution)/shard_map/psum | solution.py:15
  533.1 144.9 %reduce-scatter.29.cloned.1.call-start = ((), (), s32[]{:S(2)}) async-start(), calls=%async_computation.25 | async-start | bytes 1474560
  575.8 132.4 %reduce-scatter.27.cloned.1.call-start = ((), (), s32[]{:S(2)}) async-start(), calls=%async_computation.24 | async-start | bytes 1474560
  616.5 122.5 %reduce-scatter.19.cloned.1.call-start = ((), (), s32[]{:S(2)}) async-start(), calls=%async_computation.20 | async-start | bytes 1474560 | tf_op jit(solution)/shard_map/reduce_scatter | solution.py:298
  619.8 205.5 %reduce-scatter.21.cloned.1.call-start = ((), (), s32[]{:S(2)}) async-start(), calls=%async_computation.21 | async-start | bytes 5898240 | tf_op jit(solution)/shard_map/reduce_scatter | solution.py:310
  627.4 286.0 %reduce-scatter.23.cloned.1.call-start = ((), (), s32[]{:S(2)}) async-start(), calls=%async_computation.22 | async-start | bytes 5898240 | tf_op jit(solution)/shard_map/reduce_scatter | solution.py:316
  634.4 279.0 %copy-start.14 = (f32[2,256]{1,0:T(2,128)S(1)}, f32[2,256]{1,0:T(2,128)}, u32[]{:S(2)}) copy-start(f32[2,256]{1,0:T(2,128)} %get-tuple-element.301) | copy-start | bytes 6148
  634.4 281.6 %copy-start.22 = (bf16[192]{0:T(256)(128)(2,1)S(1)}, bf16[192]{0:T(256)(128)(2,1)}, u32[]{:S(2)}) copy-start(bf16[192]{0:T(256)(128)(2,1)} %param.41) | copy-start | bytes 1156
  634.4 307.4 %all-reduce.27.cloned.1.call-start = ((), (), s32[]{:S(2)}) async-start(), calls=%async_computation.19 | async-start | bytes 786432 | tf_op jit(solution)/shard_map/psum | solution.py:15
  646.4 374.2 %all-reduce.29.cloned.1.call-start = ((), (), s32[]{:S(2)}) async-start(), calls=%async_computation.26 | async-start | bytes 6881280 | tf_op jit(solution)/shard_map/psum | solution.py:332
  986.9 3.9 copy-start.6
  1020.7 4.7 copy-start.13
  1020.7 5.5 copy-start.12
  (13 other events, 38.3 us)
Sparse Core Ops, SparseCore 0:
  9.6 33.6 all-gather.15
  44.9 29.5 all-gather.11
  76.0 29.7 all-gather.9
  107.8 28.0 all-gather.17
  137.8 28.9 all-gather.13
  168.2 30.4 all-gather.19
  200.3 88.5 all-gather.21
  290.4 87.8 all-gather.23
  503.5 27.6 reduce-scatter.24
  533.6 36.6 reduce-scatter.16
  573.0 37.9 reduce-scatter.14
  613.7 32.6 all-reduce.24
  648.8 29.1 reduce-scatter.28
  680.3 27.8 reduce-scatter.26
  711.1 27.8 reduce-scatter.18
  741.3 83.9 reduce-scatter.20
  827.5 85.7 reduce-scatter.22
  915.6 26.2 all-reduce.26
  946.4 74.1 all-reduce.28
